TPU v7x, 32 devices: a whole 2x2x4 slice. The times are simulated.
32 devices in a mesh: gz: 2 (over y), gy: 4 (over x, core), gx: 4 (over z).
Axes of the slice: x: 2, y: 2, z: 4, core: 2. Of those that a mesh axis runs over, the one named last changes fastest.
Arguments:
- labels: int32 [2, 32, 512], P('gz', 'gy', 'gx'), may hold values from 0 to 7
- tissue_tensors: float32 [6, 8], replicated, as said below
- electrodes: int32 [2, 64], replicated, may hold values from 0 to 32767, as said below
- initial: float32 [64, 2, 32, 512], P(None, 'gz', 'gy', 'gx'), may hold values from -4 to 4
Outputs:
- solution: float32 [64, 2, 32, 512], P(None, 'gz', 'gy', 'gx')
- residual: float32 [64, 2, 32, 512], P(None, 'gz', 'gy', 'gx')
Inputs may be any that keep to these rules, and one draw needn't show every extreme that they name: `tissue_tensors`: the tensors are symmetric and positive definite: each off-diagonal component is at most 0.3 times the geometric mean of its two diagonal components. `electrodes`: all 128 voxel indices are distinct; voxel (z, y, x) has index (z * 32 + y) * 512 + x.
All inputs are finite; a program needn't handle non-finite values.
Results may differ from a plain program's by a relative error of at most 0.0003.
Values sent between devices are 32-bit elements; how exact they have to be, the bound alone decides.
A program may use at most 64 MiB of HBM per device.

v0:
```python
import jax
import jax.numpy as jnp
from jax import lax
from jax.sharding import PartitionSpec as P

ITERS = 2


def from_behind(value, axis, steps):
    count = lax.axis_size(axis)
    initial, last = (max(0, -steps), min(count, count - steps))
    return lax.ppermute(value, axis, [(source, source + steps) for source in range(initial, last)])


def padded_2(block, sides, width):
    for axis, dim in sides:
        count = lax.axis_size(axis)
        forward = [(i, i + 1) for i in range(count - 1)]
        backward = [(target, source) for source, target in forward]
        low = lax.ppermute(
            lax.slice_in_dim(block, block.shape[dim] - width, None, axis=dim), axis, forward
        )
        high = lax.ppermute(lax.slice_in_dim(block, 0, width, axis=dim), axis, backward)
        block = jnp.concatenate([low, block, high], axis=dim)
    return block


def tensor_lookup(labels, table):
    result = jnp.zeros((6,) + labels.shape, jnp.float32)
    for tissue in range(table.shape[1]):
        result = result + jnp.where(
            labels[None] == tissue, table[:, tissue][:, None, None, None], jnp.float32(0.0)
        )
    return result


def flux_terms(tensor, grad_x, grad_y, grad_z):
    flux_x = tensor[0] * grad_x + tensor[3] * grad_y + tensor[4] * grad_z
    flux_y = tensor[3] * grad_x + tensor[1] * grad_y + tensor[5] * grad_z
    flux_z = tensor[4] * grad_x + tensor[5] * grad_y + tensor[2] * grad_z
    return (flux_x, flux_y, flux_z)


def lower_box(tensor):
    below_z = from_behind(tensor, "gz", 1)
    below_y = from_behind(tensor[:, :, -1:], "gy", 1)
    below_x = from_behind(tensor[:, :, :, -1:], "gx", 1)
    inner = jnp.concatenate([below_x, tensor], axis=3)
    side_y = jnp.pad(below_y, ((0, 0), (0, 0), (0, 0), (1, 0)))
    inner = jnp.concatenate([side_y, inner], axis=2)
    side_z = jnp.pad(below_z, ((0, 0), (0, 0), (1, 0), (1, 0)))
    return jnp.concatenate([side_z, inner], axis=1)


def operate_faces(direction, tensor_box):
    padded = padded_2(direction, (("gz", 1), ("gy", 2), ("gx", 3)), 1)
    centre = padded[:, :-1, :-1, :-1]
    grad_z = padded[:, 1:, :-1, :-1] - centre
    grad_y = padded[:, :-1, 1:, :-1] - centre
    grad_x = padded[:, :-1, :-1, 1:] - centre
    flux_x, flux_y, flux_z = flux_terms(tensor_box, grad_x, grad_y, grad_z)
    return (
        flux_z[:, :-1, 1:, 1:]
        - flux_z[:, 1:, 1:, 1:]
        + (flux_y[:, 1:, :-1, 1:] - flux_y[:, 1:, 1:, 1:])
        + (flux_x[:, 1:, 1:, :-1] - flux_x[:, 1:, 1:, 1:])
    )


def gram_of(first, second):
    leads = first.shape[0]
    return lax.dot_general(
        first.reshape(leads, -1),
        second.reshape(leads, -1),
        (((1,), (1,)), ((), ())),
        precision=lax.Precision.HIGHEST,
        preferred_element_type=jnp.float32,
    )


def combine_rows(coef, field):
    leads = field.shape[0]
    return jnp.dot(
        coef.T,
        field.reshape(leads, -1),
        precision=lax.Precision.HIGHEST,
        preferred_element_type=jnp.float32,
    ).reshape(field.shape)


def factor_solve(matrix, target):
    factor = jnp.linalg.cholesky(matrix)
    halfway = lax.linalg.triangular_solve(factor, target, left_side=True, lower=True)
    return lax.linalg.triangular_solve(
        factor, halfway, left_side=True, lower=True, transpose_a=True
    )


def body(labels, tissue_tensors, electrodes, initial):
    cells_z, cells_y, cells_x = labels.shape
    rows_all = cells_y * lax.axis_size("gy")
    cols_all = cells_x * lax.axis_size("gx")
    depth_ids = lax.axis_index("gz") * cells_z + lax.broadcasted_iota(jnp.int32, labels.shape, 0)
    row_ids = lax.axis_index("gy") * cells_y + lax.broadcasted_iota(jnp.int32, labels.shape, 1)
    col_ids = lax.axis_index("gx") * cells_x + lax.broadcasted_iota(jnp.int32, labels.shape, 2)
    voxel_id = (depth_ids * rows_all + row_ids) * cols_all + col_ids
    sources = (voxel_id[None] == electrodes[0][:, None, None, None]).astype(jnp.float32) - (
        voxel_id[None] == electrodes[1][:, None, None, None]
    ).astype(jnp.float32)
    tensor = tensor_lookup(labels, tissue_tensors)
    tensor_box = lower_box(tensor)

    def operate(field):
        return operate_faces(field, tensor_box)

    solution = initial
    residual = sources - operate(initial)
    direction = residual
    rr_now = lax.psum(gram_of(residual, residual), ("gz", "gy", "gx"))
    for iteration in range(ITERS):
        image = operate(direction)
        curve = lax.psum(gram_of(direction, image), ("gz", "gy", "gx"))
        step_coef = factor_solve(curve, rr_now)
        solution = solution + combine_rows(step_coef, direction)
        residual = residual - combine_rows(step_coef, image)
        if iteration + 1 < ITERS:
            rr_next = lax.psum(gram_of(residual, residual), ("gz", "gy", "gx"))
            beta_coef = factor_solve(rr_now, rr_next)
            direction = residual + combine_rows(beta_coef, direction)
            rr_now = rr_next
    return (solution, residual)


def solution(mesh):
    placed = (P("gz", "gy", "gx"), P(), P(), P(None, "gz", "gy", "gx"))
    return jax.shard_map(
        body,
        mesh=mesh,
        in_specs=placed,
        out_specs=(P(None, "gz", "gy", "gx"), P(None, "gz", "gy", "gx")),
        check_vma=False,
    )
```

profile of v0, /device:TPU:0, one launch (start us, length us, event | category | flops | bytes accessed | tf_op | source)
XLA Modules:
  0.0 279.7 jit_solution(1200948065979888118)
XLA Ops:
  1.7 4.9 %collective-permute-start.3 = (f32[64,1,8,128]{3,0,2,1:T(8,128)S(1)}, f32[64,1,8,128]{3,0,2,1:T(8,128)S(1)}, u32[]{:S(2)}, u32[]{:S(2)}) collective-permute-start(f32[64,1,8,128]{3,0,2,1:T(8,128)S(1)} %copy.64), channel_id=1, source_target_pairs={{0,16},{1,17},{2,18},{3,19},{4,20},{5,21},{6,22},{7,23},{8,24},{9,... | collective-permute-start | bytes 786440 | tf_op jit(solution)/shard_map/ppermute | solution.py:20
  6.6 1.3 collective-permute-start.4
  10.0 4.6 %collective-permute-start = (f32[6,1,8,128]{3,2,1,0:T(8,128)S(1)}, f32[6,1,8,128]{3,2,1,0:T(8,128)S(1)}, u32[]{:S(2)}, u32[]{:S(2)}) collective-permute-start(f32[6,1,8,128]{3,2,1,0:T(8,128)S(1)} %select_add_fusion), channel_id=1, source_target_pairs={{0,16},{1,17},{2,18},{3,19},{4,20},{5,21},{6,22},{7,23},{8,24},{9,... | collective-permute-start | bytes 73736 | tf_op jit(solution)/shard_map/ppermute | solution.py:12
  14.6 3.5 %collective-permute-start.2 = (f32[6,1,8,1]{3,2,1,0:T(8,128)S(1)}, f32[6,1,8,1]{3,2,1,0:T(8,128)S(1)}, u32[]{:S(2)}, u32[]{:S(2)}) collective-permute-start(f32[6,1,8,1]{3,2,1,0:T(8,128)S(1)} %slice.282), channel_id=1, source_target_pairs={{0,1},{1,2},{2,3},{4,5},{5,6},{6,7},{8,9},{9,10},{10,11},{12,13},{... | collective-permute-start | bytes 584 | tf_op jit(solution)/shard_map/ppermute | solution.py:12
  20.4 4.1 %collective-permute-start.5 = (f32[64,3,1,128]{3,0,2,1:T(8,128)S(1)}, f32[64,3,1,128]{3,0,2,1:T(8,128)S(1)}, u32[]{:S(2)}, u32[]{:S(2)}) collective-permute-start(f32[64,3,1,128]{3,0,2,1:T(8,128)S(1)} %get-tuple-element.43), channel_id=1, source_target_pairs={{0,4},{4,8},{8,12},{1,5},{5,9},{9,13},{2,6},{6,10},{10,14},{3,7},{... | collective-permute-start | bytes 294920 | tf_op jit(solution)/shard_map/ppermute | solution.py:20
  24.6 1.3 collective-permute-start.6
  26.1 1.7 collective-permute-done.6
  29.2 3.5 %collective-permute-start.8 = (f32[64,3,10,1]{0,3,2,1:T(1,128)}, f32[64,3,10,1]{0,3,2,1:T(1,128)S(1)}, u32[]{:S(2)}, u32[]{:S(2)}) collective-permute-start(f32[64,3,10,1]{0,3,2,1:T(1,128)} %copy.52), channel_id=1, source_target_pairs={{0,1},{1,2},{2,3},{4,5},{5,6},{6,7},{8,9},{9,10},{10,11},{12,13},{... | collective-permute-start | bytes 23048 | tf_op jit(solution)/shard_map/ppermute | solution.py:20
  33.6 1.3 collective-permute-start.7
  34.9 1.3 copy.53
  36.3 1.8 maximum_maximum_fusion
  39.3 1.3 copy.51
  40.6 1.5 multiply_add_fusion.8
  43.2 1.3 collective-permute-start.10
  44.5 4.6 %collective-permute-start.9 = (f32[64,1,8,128]{3,0,2,1:T(8,128)S(1)}, f32[64,1,8,128]{3,0,2,1:T(8,128)S(1)}, u32[]{:S(2)}, u32[]{:S(2)}) collective-permute-start(f32[64,1,8,128]{3,0,2,1:T(8,128)S(1)} %fusion.21), channel_id=1, source_target_pairs={{0,16},{1,17},{2,18},{3,19},{4,20},{5,21},{6,22},{7,23},{8,24},{9,... | collective-permute-start | bytes 786440 | tf_op jit(solution)/shard_map/ppermute | solution.py:20
  49.1 4.9 %collective-permute-done.10 = f32[64,1,8,128]{3,0,2,1:T(8,128)S(1)} collective-permute-done((f32[64,1,8,128]{3,0,2,1:T(8,128)S(1)}, f32[64,1,8,128]{3,0,2,1:T(8,128)S(1)}, u32[]{:S(2)}, u32[]{:S(2)}) %collective-permute-start.10) | collective-permute-done | bytes 262176 | tf_op jit(solution)/shard_map/ppermute | solution.py:23
  54.0 1.7 collective-permute-done.9
  55.7 2.2 collective-permute-start.11
  57.9 1.3 collective-permute-start.12
  59.2 1.9 collective-permute-done.12
  61.8 3.4 %collective-permute-start.14 = (f32[64,3,10,1]{0,3,2,1:T(1,128)S(1)}, f32[64,3,10,1]{0,3,2,1:T(1,128)S(1)}, u32[]{:S(2)}, u32[]{:S(2)}) collective-permute-start(f32[64,3,10,1]{0,3,2,1:T(1,128)S(1)} %copy.56), channel_id=1, source_target_pairs={{0,1},{1,2},{2,3},{4,5},{5,6},{6,7},{8,9},{9,10},{10,11},{12,13},{... | collective-permute-start | bytes 23048 | tf_op jit(solution)/shard_map/ppermute | solution.py:20
  68.6 1.3 copy.57
  70.0 1.8 maximum_maximum_fusion.1
  71.8 1.5 collective-permute-done.13
  73.3 2.0 copy.55
  75.3 1.5 multiply_add_fusion.5
  78.5 42.6 %all-reduce.2 = (f32[64,64]{0,1:T(8,128)S(1)}, f32[64,64]{0,1:T(8,128)S(1)}) all-reduce(f32[64,64]{0,1:T(8,128)S(1)} %copy-done.22, f32[64,64]{0,1:T(8,128)S(1)} %convolution_bitcast_fusion.11), channel_id=1, replica_groups=mesh['gz'=2,'gy'=4,'gx'=4] {'gz','gy','gx'}, use_global_device_ids=true, to_apply=%region_3.5 | all-reduce | flops 8192 | bytes 65536 | tf_op jit(solution)/shard_map/psum | solution.py:119
  121.3 5.8 %cholesky.70 = f32[64,64]{1,0:T(8,128)S(1)} custom-call(f32[64,64]{1,0:T(8,128)S(1)} %get-tuple-element.61), custom_call_target="Cholesky" | custom-call | tf_op jit(solution)/shard_map/jit(cholesky)/cholesky | solution.py:92
  128.5 4.9 %custom-call.15 = f32[1,64,64]{1,2,0:T(8,128)S(1)} custom-call(f32[1,64,64]{2,1,0:T(8,128)S(1)} %fusion.34), custom_call_target="InvertDiagBlocksLowerTriangular" | custom-call | tf_op jit(solution)/shard_map/triangular_solve/custom-call.2 | solution.py:94
  133.4 5.9 %cholesky.59 = f32[64,64]{1,0:T(8,128)S(1)} custom-call(f32[64,64]{1,0:T(8,128)S(1)} %get-tuple-element.62), custom_call_target="Cholesky" | custom-call | tf_op jit(solution)/shard_map/jit(cholesky)/cholesky | solution.py:92
  140.6 4.9 %custom-call.13 = f32[1,64,64]{1,2,0:T(8,128)S(1)} custom-call(f32[1,64,64]{2,1,0:T(8,128)S(1)} %fusion.33), custom_call_target="InvertDiagBlocksLowerTriangular" | custom-call | tf_op jit(solution)/shard_map/triangular_solve/custom-call.2 | solution.py:94
  146.8 38.9 %psum.30 = f32[64,64]{1,0:T(8,128)S(1)} all-reduce(f32[64,64]{1,0:T(8,128)S(1)} %convolution_bitcast_fusion.9), channel_id=1, replica_groups=mesh['gz'=2,'gy'=4,'gx'=4] {'gz','gy','gx'}, use_global_device_ids=true, to_apply=%region_4.8 | all-reduce | flops 4096 | bytes 32768 | tf_op jit(solution)/shard_map/psum | solution.py:127
  186.6 4.2 %collective-permute-start.15 = (f32[64,1,8,128]{3,0,2,1:T(8,128)S(1)}, f32[64,1,8,128]{3,0,2,1:T(8,128)S(1)}, u32[]{:S(2)}, u32[]{:S(2)}) collective-permute-start(f32[64,1,8,128]{3,0,2,1:T(8,128)S(1)} %fusion.6), channel_id=1, source_target_pairs={{0,16},{1,17},{2,18},{3,19},{4,20},{5,21},{6,22},{7,23},{8,24},{9,... | collective-permute-start | bytes 786440 | tf_op jit(solution)/shard_map/ppermute | solution.py:20
  190.9 1.3 collective-permute-start.16
  192.2 3.9 %collective-permute-done.15 = f32[64,1,8,128]{3,0,2,1:T(8,128)S(1)} collective-permute-done((f32[64,1,8,128]{3,0,2,1:T(8,128)S(1)}, f32[64,1,8,128]{3,0,2,1:T(8,128)S(1)}, u32[]{:S(2)}, u32[]{:S(2)}) %collective-permute-start.15) | collective-permute-done | bytes 262176 | tf_op jit(solution)/shard_map/ppermute | solution.py:20
  196.0 4.1 %collective-permute-done.16 = f32[64,1,8,128]{3,0,2,1:T(8,128)S(1)} collective-permute-done((f32[64,1,8,128]{3,0,2,1:T(8,128)S(1)}, f32[64,1,8,128]{3,0,2,1:T(8,128)S(1)}, u32[]{:S(2)}, u32[]{:S(2)}) %collective-permute-start.16) | collective-permute-done | bytes 262176 | tf_op jit(solution)/shard_map/ppermute | solution.py:23
  200.2 1.3 collective-permute-start.17
  201.5 1.3 collective-permute-start.18
  202.8 2.9 %collective-permute-done.18 = f32[64,3,1,128]{3,0,2,1:T(8,128)S(1)} collective-permute-done((f32[64,3,1,128]{3,0,2,1:T(8,128)S(1)}, f32[64,3,1,128]{3,0,2,1:T(8,128)S(1)}, u32[]{:S(2)}, u32[]{:S(2)}) %collective-permute-start.18) | collective-permute-done | bytes 98336 | tf_op jit(solution)/shard_map/ppermute | solution.py:23
  207.2 3.3 %collective-permute-start.20 = (f32[64,3,10,1]{0,3,2,1:T(1,128)S(1)}, f32[64,3,10,1]{0,3,2,1:T(1,128)S(1)}, u32[]{:S(2)}, u32[]{:S(2)}) collective-permute-start(f32[64,3,10,1]{0,3,2,1:T(1,128)S(1)} %copy.73), channel_id=1, source_target_pairs={{0,1},{1,2},{2,3},{4,5},{5,6},{6,7},{8,9},{9,10},{10,11},{12,13},{... | collective-permute-start | bytes 23048 | tf_op jit(solution)/shard_map/ppermute | solution.py:20
  213.6 1.3 copy.74
  214.9 1.9 maximum_maximum_fusion.2
  216.8 1.4 collective-permute-done.19
  218.2 2.0 copy.72
  220.3 1.6 multiply_add_fusion.2
  223.5 40.5 %psum.31 = f32[64,64]{0,1:T(8,128)S(1)} all-reduce(f32[64,64]{0,1:T(8,128)S(1)} %convolution_bitcast_fusion.8), channel_id=1, replica_groups=mesh['gz'=2,'gy'=4,'gx'=4] {'gz','gy','gx'}, use_global_device_ids=true, to_apply=%region_5.9 | all-reduce | flops 4096 | bytes 32768 | tf_op jit(solution)/shard_map/psum | solution.py:122
  264.1 5.8 %cholesky.81 = f32[64,64]{1,0:T(8,128)S(1)} custom-call(f32[64,64]{1,0:T(8,128)S(1)} %fusion.39), custom_call_target="Cholesky" | custom-call | tf_op jit(solution)/shard_map/jit(cholesky)/cholesky | solution.py:92
  271.3 4.9 %custom-call.17 = f32[1,64,64]{1,2,0:T(8,128)S(1)} custom-call(f32[1,64,64]{2,1,0:T(8,128)S(1)} %fusion.35), custom_call_target="InvertDiagBlocksLowerTriangular" | custom-call | tf_op jit(solution)/shard_map/triangular_solve/custom-call.2 | solution.py:94
  (132 shorter events, 32.0 us)
Async XLA Ops:
  0.6 19.7 %copy-start = (f32[64,1,8,128]{3,2,1,0:T(8,128)S(1)}, f32[64,1,8,128]{3,2,1,0:T(8,128)}, u32[]{:S(2)}) copy-start(f32[64,1,8,128]{3,2,1,0:T(8,128)} %param.12) | copy-start | bytes 786436
  1.7 18.6 %collective-permute-start.3 = (f32[64,1,8,128]{3,0,2,1:T(8,128)S(1)}, f32[64,1,8,128]{3,0,2,1:T(8,128)S(1)}, u32[]{:S(2)}, u32[]{:S(2)}) collective-permute-start(f32[64,1,8,128]{3,0,2,1:T(8,128)S(1)} %copy.64), channel_id=1, source_target_pairs={{0,16},{1,17},{2,18},{3,19},{4,20},{5,21},{6,22},{7,23},{8,24},{9,... | collective-permute-start | bytes 786440 | tf_op jit(solution)/shard_map/ppermute | solution.py:20
  6.6 13.8 %collective-permute-start.4 = (f32[64,1,8,128]{3,0,2,1:T(8,128)S(1)}, f32[64,1,8,128]{3,0,2,1:T(8,128)S(1)}, u32[]{:S(2)}, u32[]{:S(2)}) collective-permute-start(f32[64,1,8,128]{3,0,2,1:T(8,128)S(1)} %copy.64), channel_id=1, source_target_pairs={{16,0},{17,1},{18,2},{19,3},{20,4},{21,5},{22,6},{23,7},{24,8},{25... | collective-permute-start | bytes 786440 | tf_op jit(solution)/shard_map/ppermute | solution.py:23
  10.0 15.9 %collective-permute-start = (f32[6,1,8,128]{3,2,1,0:T(8,128)S(1)}, f32[6,1,8,128]{3,2,1,0:T(8,128)S(1)}, u32[]{:S(2)}, u32[]{:S(2)}) collective-permute-start(f32[6,1,8,128]{3,2,1,0:T(8,128)S(1)} %select_add_fusion), channel_id=1, source_target_pairs={{0,16},{1,17},{2,18},{3,19},{4,20},{5,21},{6,22},{7,23},{8,24},{9,... | collective-permute-start | bytes 73736 | tf_op jit(solution)/shard_map/ppermute | solution.py:12
  14.6 11.2 %collective-permute-start.2 = (f32[6,1,8,1]{3,2,1,0:T(8,128)S(1)}, f32[6,1,8,1]{3,2,1,0:T(8,128)S(1)}, u32[]{:S(2)}, u32[]{:S(2)}) collective-permute-start(f32[6,1,8,1]{3,2,1,0:T(8,128)S(1)} %slice.282), channel_id=1, source_target_pairs={{0,1},{1,2},{2,3},{4,5},{5,6},{6,7},{8,9},{9,10},{10,11},{12,13},{... | collective-permute-start | bytes 584 | tf_op jit(solution)/shard_map/ppermute | solution.py:12
  18.1 7.8 %collective-permute-start.1 = (f32[6,1,1,128]{3,2,1,0:T(1,128)S(1)}, f32[6,1,1,128]{3,2,1,0:T(1,128)S(1)}, u32[]{:S(2)}, u32[]{:S(2)}) collective-permute-start(f32[6,1,1,128]{3,2,1,0:T(1,128)S(1)} %slice.281), channel_id=1, source_target_pairs={{0,4},{4,8},{8,12},{1,5},{5,9},{9,13},{2,6},{6,10},{10,14},{3,7},{... | collective-permute-start | bytes 9224 | tf_op jit(solution)/shard_map/ppermute | solution.py:12
  20.4 5.6 %collective-permute-start.5 = (f32[64,3,1,128]{3,0,2,1:T(8,128)S(1)}, f32[64,3,1,128]{3,0,2,1:T(8,128)S(1)}, u32[]{:S(2)}, u32[]{:S(2)}) collective-permute-start(f32[64,3,1,128]{3,0,2,1:T(8,128)S(1)} %get-tuple-element.43), channel_id=1, source_target_pairs={{0,4},{4,8},{8,12},{1,5},{5,9},{9,13},{2,6},{6,10},{10,14},{3,7},{... | collective-permute-start | bytes 294920 | tf_op jit(solution)/shard_map/ppermute | solution.py:20
  24.6 3.2 %collective-permute-start.6 = (f32[64,3,1,128]{3,0,2,1:T(8,128)S(1)}, f32[64,3,1,128]{3,0,2,1:T(8,128)S(1)}, u32[]{:S(2)}, u32[]{:S(2)}) collective-permute-start(f32[64,3,1,128]{3,0,2,1:T(8,128)S(1)} %get-tuple-element.44), channel_id=1, source_target_pairs={{4,0},{8,4},{12,8},{5,1},{9,5},{13,9},{6,2},{10,6},{14,10},{7,3},{... | collective-permute-start | bytes 294920 | tf_op jit(solution)/shard_map/ppermute | solution.py:23
  29.2 5.8 %collective-permute-start.8 = (f32[64,3,10,1]{0,3,2,1:T(1,128)}, f32[64,3,10,1]{0,3,2,1:T(1,128)S(1)}, u32[]{:S(2)}, u32[]{:S(2)}) collective-permute-start(f32[64,3,10,1]{0,3,2,1:T(1,128)} %copy.52), channel_id=1, source_target_pairs={{0,1},{1,2},{2,3},{4,5},{5,6},{6,7},{8,9},{9,10},{10,11},{12,13},{... | collective-permute-start | bytes 23048 | tf_op jit(solution)/shard_map/ppermute | solution.py:20
  33.3 8.8 %copy-start.8 = (f32[2,9,129]{2,1,0:T(8,128)}, f32[2,9,129]{2,1,0:T(8,128)S(1)}, u32[]{:S(2)}) copy-start(f32[2,9,129]{2,1,0:T(8,128)S(1)} %get-tuple-element.45) | copy-start | bytes 27868
  33.3 8.8 %copy-start.11 = (f32[2,9,129]{2,1,0:T(8,128)}, f32[2,9,129]{2,1,0:T(8,128)S(1)}, u32[]{:S(2)}) copy-start(f32[2,9,129]{2,1,0:T(8,128)S(1)} %get-tuple-element.46) | copy-start | bytes 27868
  33.3 43.5 %copy-start.1 = (f32[2,9,129]{2,1,0:T(8,128)}, f32[2,9,129]{2,1,0:T(8,128)S(1)}, u32[]{:S(2)}) copy-start(f32[2,9,129]{2,1,0:T(8,128)S(1)} %get-tuple-element.49) | copy-start | bytes 27868
  33.3 43.5 %copy-start.3 = (f32[2,9,129]{2,1,0:T(8,128)}, f32[2,9,129]{2,1,0:T(8,128)S(1)}, u32[]{:S(2)}) copy-start(f32[2,9,129]{2,1,0:T(8,128)S(1)} %get-tuple-element.50) | copy-start | bytes 27868
  33.6 5.6 %collective-permute-start.7 = (f32[64,3,10,1]{0,3,2,1:T(1,128)S(1)}, f32[64,3,10,1]{0,3,2,1:T(1,128)S(1)}, u32[]{:S(2)}, u32[]{:S(2)}) collective-permute-start(f32[64,3,10,1]{0,3,2,1:T(1,128)S(1)} %copy.50), channel_id=1, source_target_pairs={{1,0},{2,1},{3,2},{5,4},{6,5},{7,6},{9,8},{10,9},{11,10},{13,12},{... | collective-permute-start | bytes 23048 | tf_op jit(solution)/shard_map/ppermute | solution.py:23
  36.3 4.3 %copy-start.17 = (f32[2,9,129]{2,1,0:T(8,128)S(1)}, f32[2,9,129]{2,1,0:T(8,128)}, u32[]{:S(2)}) copy-start(f32[2,9,129]{2,1,0:T(8,128)} %get-tuple-element.48) | copy-start | bytes 27868
  40.6 1.5 copy-start.14
  43.2 10.8 %collective-permute-start.10 = (f32[64,1,8,128]{3,0,2,1:T(8,128)S(1)}, f32[64,1,8,128]{3,0,2,1:T(8,128)S(1)}, u32[]{:S(2)}, u32[]{:S(2)}) collective-permute-start(f32[64,1,8,128]{3,0,2,1:T(8,128)S(1)} %fusion.21), channel_id=1, source_target_pairs={{16,0},{17,1},{18,2},{19,3},{20,4},{21,5},{22,6},{23,7},{24,8},{25... | collective-permute-start | bytes 786440 | tf_op jit(solution)/shard_map/ppermute | solution.py:23
  44.5 11.2 %collective-permute-start.9 = (f32[64,1,8,128]{3,0,2,1:T(8,128)S(1)}, f32[64,1,8,128]{3,0,2,1:T(8,128)S(1)}, u32[]{:S(2)}, u32[]{:S(2)}) collective-permute-start(f32[64,1,8,128]{3,0,2,1:T(8,128)S(1)} %fusion.21), channel_id=1, source_target_pairs={{0,16},{1,17},{2,18},{3,19},{4,20},{5,21},{6,22},{7,23},{8,24},{9,... | collective-permute-start | bytes 786440 | tf_op jit(solution)/shard_map/ppermute | solution.py:20
  55.7 3.5 %collective-permute-start.11 = (f32[64,3,1,128]{3,0,2,1:T(8,128)S(1)}, f32[64,3,1,128]{3,0,2,1:T(8,128)S(1)}, u32[]{:S(2)}, u32[]{:S(2)}) collective-permute-start(f32[64,3,1,128]{3,0,2,1:T(8,128)S(1)} %get-tuple-element.41), channel_id=1, source_target_pairs={{0,4},{4,8},{8,12},{1,5},{5,9},{9,13},{2,6},{6,10},{10,14},{3,7},{... | collective-permute-start | bytes 294920 | tf_op jit(solution)/shard_map/ppermute | solution.py:20
  57.9 3.2 %collective-permute-start.12 = (f32[64,3,1,128]{3,0,2,1:T(8,128)S(1)}, f32[64,3,1,128]{3,0,2,1:T(8,128)S(1)}, u32[]{:S(2)}, u32[]{:S(2)}) collective-permute-start(f32[64,3,1,128]{3,0,2,1:T(8,128)S(1)} %get-tuple-element.42), channel_id=1, source_target_pairs={{4,0},{8,4},{12,8},{5,1},{9,5},{13,9},{6,2},{10,6},{14,10},{7,3},{... | collective-permute-start | bytes 294920 | tf_op jit(solution)/shard_map/ppermute | solution.py:23
  61.8 6.8 %collective-permute-start.14 = (f32[64,3,10,1]{0,3,2,1:T(1,128)S(1)}, f32[64,3,10,1]{0,3,2,1:T(1,128)S(1)}, u32[]{:S(2)}, u32[]{:S(2)}) collective-permute-start(f32[64,3,10,1]{0,3,2,1:T(1,128)S(1)} %copy.56), channel_id=1, source_target_pairs={{0,1},{1,2},{2,3},{4,5},{5,6},{6,7},{8,9},{9,10},{10,11},{12,13},{... | collective-permute-start | bytes 23048 | tf_op jit(solution)/shard_map/ppermute | solution.py:20
  67.3 5.9 %collective-permute-start.13 = (f32[64,3,10,1]{0,3,2,1:T(1,128)}, f32[64,3,10,1]{0,3,2,1:T(1,128)}, u32[]{:S(2)}, u32[]{:S(2)}) collective-permute-start(f32[64,3,10,1]{0,3,2,1:T(1,128)} %copy.54), channel_id=1, source_target_pairs={{1,0},{2,1},{3,2},{5,4},{6,5},{7,6},{9,8},{10,9},{11,10},{13,12},{... | collective-permute-start | bytes 23048 | tf_op jit(solution)/shard_map/ppermute | solution.py:23
  75.3 1.5 copy-start.9
  75.3 1.5 copy-start.12
  75.3 1.5 copy-start.15
  77.5 1.0 copy-start.22
  146.0 40.7 %copy-start.18 = (f32[64,64,1]{0,1,2:T(8,128)}, f32[64,64,1]{0,1,2:T(8,128)S(1)}, u32[]{:S(2)}) copy-start(f32[64,64,1]{0,1,2:T(8,128)S(1)} %convolution_bitcast_fusion.7) | copy-start | bytes 49156
  185.6 0.6 copy-start.20
  186.6 9.4 %collective-permute-start.15 = (f32[64,1,8,128]{3,0,2,1:T(8,128)S(1)}, f32[64,1,8,128]{3,0,2,1:T(8,128)S(1)}, u32[]{:S(2)}, u32[]{:S(2)}) collective-permute-start(f32[64,1,8,128]{3,0,2,1:T(8,128)S(1)} %fusion.6), channel_id=1, source_target_pairs={{0,16},{1,17},{2,18},{3,19},{4,20},{5,21},{6,22},{7,23},{8,24},{9,... | collective-permute-start | bytes 786440 | tf_op jit(solution)/shard_map/ppermute | solution.py:20
  190.9 9.3 %collective-permute-start.16 = (f32[64,1,8,128]{3,0,2,1:T(8,128)S(1)}, f32[64,1,8,128]{3,0,2,1:T(8,128)S(1)}, u32[]{:S(2)}, u32[]{:S(2)}) collective-permute-start(f32[64,1,8,128]{3,0,2,1:T(8,128)S(1)} %fusion.6), channel_id=1, source_target_pairs={{16,0},{17,1},{18,2},{19,3},{20,4},{21,5},{22,6},{23,7},{24,8},{25... | collective-permute-start | bytes 786440 | tf_op jit(solution)/shard_map/ppermute | solution.py:23
  200.2 2.6 collective-permute-start.17
  201.5 4.3 %collective-permute-start.18 = (f32[64,3,1,128]{3,0,2,1:T(8,128)S(1)}, f32[64,3,1,128]{3,0,2,1:T(8,128)S(1)}, u32[]{:S(2)}, u32[]{:S(2)}) collective-permute-start(f32[64,3,1,128]{3,0,2,1:T(8,128)S(1)} %get-tuple-element.40), channel_id=1, source_target_pairs={{4,0},{8,4},{12,8},{5,1},{9,5},{13,9},{6,2},{10,6},{14,10},{7,3},{... | collective-permute-start | bytes 294920 | tf_op jit(solution)/shard_map/ppermute | solution.py:23
  202.8 2.9 %copy-start.6 = (f32[64,3,1,128]{3,0,2,1:T(8,128)}, f32[64,3,1,128]{3,0,2,1:T(8,128)S(1)}, u32[]{:S(2)}) copy-start(f32[64,3,1,128]{3,0,2,1:T(8,128)S(1)} %collective-permute-done.17) | copy-start | bytes 294916
  205.7 0.6 copy-start.7
  207.2 6.4 %collective-permute-start.20 = (f32[64,3,10,1]{0,3,2,1:T(1,128)S(1)}, f32[64,3,10,1]{0,3,2,1:T(1,128)S(1)}, u32[]{:S(2)}, u32[]{:S(2)}) collective-permute-start(f32[64,3,10,1]{0,3,2,1:T(1,128)S(1)} %copy.73), channel_id=1, source_target_pairs={{0,1},{1,2},{2,3},{4,5},{5,6},{6,7},{8,9},{9,10},{10,11},{12,13},{... | collective-permute-start | bytes 23048 | tf_op jit(solution)/shard_map/ppermute | solution.py:20
  212.3 5.9 %collective-permute-start.19 = (f32[64,3,10,1]{0,3,2,1:T(1,128)}, f32[64,3,10,1]{0,3,2,1:T(1,128)}, u32[]{:S(2)}, u32[]{:S(2)}) collective-permute-start(f32[64,3,10,1]{0,3,2,1:T(1,128)} %copy.71), channel_id=1, source_target_pairs={{1,0},{2,1},{3,2},{5,4},{6,5},{7,6},{9,8},{10,9},{11,10},{13,12},{... | collective-permute-start | bytes 23048 | tf_op jit(solution)/shard_map/ppermute | solution.py:23
  220.3 1.6 copy-start.2
  220.3 1.6 copy-start.4
  220.3 1.6 copy-start.10
  220.3 1.6 copy-start.13
  220.3 1.6 copy-start.16
  222.6 53.6 %copy-start.21 = (f32[64,64]{1,0:T(8,128)S(1)}, f32[64,64]{1,0:T(8,128)}, u32[]{:S(2)}) copy-start(f32[64,64]{1,0:T(8,128)} %copy-done.20) | copy-start | bytes 49156
  223.4 54.6 %copy-start.5 = (f32[64,1,8,128]{3,2,0,1:T(8,128)S(1)}, f32[64,1,8,128]{3,2,0,1:T(8,128)}, u32[]{:S(2)}) copy-start(f32[64,1,8,128]{3,2,0,1:T(8,128)} %copy.77) | copy-start | bytes 786436
  264.0 14.4 %copy-start.19 = (f32[64,64,1]{0,1,2:T(8,128)S(1)}, f32[64,64,1]{0,1,2:T(8,128)}, u32[]{:S(2)}) copy-start(f32[64,64,1]{0,1,2:T(8,128)} %copy-done.18) | copy-start | bytes 49156
where the time goes:
time: 281 us; the launch traced here: 280 us
  blocking collectives  122 us (43%)
  starting transfers between devices  52.4 us (19%)
  other arithmetic  50.7 us (18%)
  waiting for transfers between devices  25.3 us (9%)
  local copies, waits for them, and re-layouts  22.4 us (8%)
  matrix products  5.49 us (2%)
    psum x1, blocking collectives, body(): rr_now = lax.psum(gram_of(residual, residual), ('gz', 'gy', 'gx'))  42.6 us
    psum x1, blocking collectives, body(): curve = lax.psum(gram_of(direction, image), ('gz', 'gy', 'gx'))  40.5 us
    psum x1, blocking collectives, body(): rr_next = lax.psum(gram_of(residual, residual), ('gz', 'gy', 'gx'))  38.9 us
    ppermute x9, starting transfers between devices, padded_2(): lax.ppermute(lax.slice_in_dim(block, block.shape[dim] - width, None, axis...  31.5 us
    ppermute x9, waiting for transfers between devices, padded_2(): lax.ppermute(lax.slice_in_dim(block, 0, width, axis=dim), axis, backward)  19.7 us
    another operation x9, other arithmetic, factor_solve(): factor = jnp.linalg.cholesky(matrix)  19.6 us
    another operation x6, other arithmetic, factor_solve(): lax.linalg.triangular_solve(factor, halfway, left_side=True, lower=True,...  16.6 us
    ppermute x9, starting transfers between devices, padded_2(): lax.ppermute(lax.slice_in_dim(block, 0, width, axis=dim), axis, backward)  11.6 us
  transfers between devices with their start and end apart: 21, of which 10 were waited for; matrix products, arithmetic and copies ran while one was open for 6% of the time, Pallas kernels for 0%

commit v1 on v0

v1 whole, which is shorter than its diff:
```python
import jax
import jax.numpy as jnp
from jax import lax
from jax.experimental import pallas as pl
from jax.experimental.pallas import tpu as pltpu
from jax.sharding import PartitionSpec as P

MESH = pl.DeviceIdType.MESH
HIGH = lax.Precision.HIGHEST
DEPTH = 3


def nt_dot(a, b):
    return lax.dot_general(
        a, b, (((1,), (1,)), ((), ())), precision=HIGH, preferred_element_type=jnp.float32
    )


def nn_dot(a, b):
    return lax.dot_general(
        a, b, (((1,), (0,)), ((), ())), precision=HIGH, preferred_element_type=jnp.float32
    )


def make_krylov(nz, ny, nx, leads, rows, cols):
    windowed = nz > DEPTH + 1
    layers = 2 * DEPTH + 1 if windowed else nz
    lead8 = leads + 8
    ext = rows + 2 * DEPTH
    top = DEPTH + rows
    if windowed:
        offsets = [d for d in range(-DEPTH, DEPTH + 1) if d]
    else:
        offsets = list(range(1, nz))
    noff = len(offsets)
    plane = nz * ny
    size = 2 * leads
    share = size // plane

    def kernel(
        table, labels, electrodes, field, base_out, gram_out,
        xe, re, qe, coef, inside, elec, xs, xr, gs, rs, zs,
        zsend, zrecv, ysend, yrecv, xsend, xrecv, asend, arecv,
    ):
        z, y, x = lax.axis_index("gz"), lax.axis_index("gy"), lax.axis_index("gx")
        me = z * ny + y
        own = DEPTH if windowed else z
        first = z - DEPTH if windowed else 0

        def plane_peer(k):
            peer = lax.rem(me + k, plane)
            return peer, {"gz": peer // ny, "gy": lax.rem(peer, ny)}

        barrier = pltpu.get_barrier_semaphore()
        for k in range(1, plane):
            pl.semaphore_signal(
                barrier, inc=1, device_id=plane_peer(k)[1], device_id_type=MESH
            )
        for k in range(1, nx):
            pl.semaphore_signal(
                barrier, inc=1, device_id={"gx": lax.rem(x + k, nx)}, device_id_type=MESH
            )

        def fill(slot, lo, hi):
            for r in range(lo, hi):
                xe[slot, r, 0:leads, 0:cols] = jnp.zeros((leads, cols), jnp.float32)
                xe[slot, r, leads:lead8, 0:cols] = jnp.full((8, cols), -1.0, jnp.float32)

        if windowed:
            for s in range(layers):

                @pl.when((first + s < 0) | (first + s >= nz))
                def _(s=s):
                    fill(s, 0, ext)

        for s in range(layers):

            @pl.when(y == 0)
            def _(s=s):
                fill(s, 0, DEPTH)

            @pl.when(y == ny - 1)
            def _(s=s):
                fill(s, top, ext)

        for side, edge in ((0, nx - 1), (1, 0)):

            @pl.when(x == edge)
            def _(side=side):
                for s in range(layers):
                    xr[side, s, 0:leads] = jnp.zeros((leads, cols), jnp.float32)
                    xr[side, s, leads:lead8] = jnp.full((8, cols), -1.0, jnp.float32)

        for r in range(rows):
            xe[own, DEPTH + r, 0:leads, 0:cols] = field[pl.ds(r, leads, stride=rows), :]
            xe[own, DEPTH + r, leads:lead8, 0:cols] = jnp.broadcast_to(
                labels[r : r + 1, :].astype(jnp.float32), (8, cols)
            )
        pl.semaphore_wait(barrier, plane - 1 + nx - 1)

        chunks = ((DEPTH, 2 * DEPTH), (top - DEPTH, top), (2 * DEPTH, top - DEPTH))

        def z_plan(i):
            d = offsets[i]
            if windowed:
                return (
                    z + d, DEPTH - d, DEPTH - d,
                    (z + d >= 0) & (z + d < nz), (z - d >= 0) & (z - d < nz),
                )
            return lax.rem(z + d, nz), z, lax.rem(z - d + nz, nz), None, None

        def when(cond, action):
            if cond is None:
                action()
            else:
                pl.when(cond)(action)

        def z_copy(i, c):
            peer, slot, _, _, _ = z_plan(i)
            lo, hi = chunks[c]
            return pltpu.make_async_remote_copy(
                src_ref=xe.at[own, lo:hi, :, 0:cols],
                dst_ref=xe.at[slot, lo:hi, :, 0:cols],
                send_sem=zsend.at[i, c],
                recv_sem=zrecv.at[i, c],
                device_id={"gz": peer},
                device_id_type=MESH,
            )

        def y_copy(i, slot, up):
            src = (top - DEPTH, top) if up else (DEPTH, 2 * DEPTH)
            dst = (0, DEPTH) if up else (top, ext)
            return pltpu.make_async_remote_copy(
                src_ref=xe.at[slot, src[0] : src[1], :, 0:cols],
                dst_ref=xe.at[slot, dst[0] : dst[1], :, 0:cols],
                send_sem=ysend.at[i, up],
                recv_sem=yrecv.at[i, up],
                device_id={"gy": y + 1 if up else y - 1},
                device_id_type=MESH,
            )

        has_low, has_high = y > 0, y < ny - 1

        def y_start(i, slot, up):
            pl.when(has_high if up else has_low)(lambda: y_copy(i, slot, up).start())

        for c in range(3):
            for i in range(noff):
                when(z_plan(i)[3], lambda i=i, c=c: z_copy(i, c).start())
        for up in (0, 1):
            y_start(noff, own, up)

        eye = lax.broadcasted_iota(jnp.int32, (leads, leads), 0) == lax.broadcasted_iota(
            jnp.int32, (leads, leads), 1
        )
        for e in range(2):
            line = electrodes[e : e + 1, :].astype(jnp.float32)
            column = jnp.sum(
                jnp.where(eye, jnp.broadcast_to(line, (leads, leads)), 0.0), axis=1, keepdims=True
            )
            elec[e] = jnp.broadcast_to(column, (leads, 2 * cols))

        for c in range(2):
            for i in range(noff):

                def arrived(i=i, c=c):
                    z_copy(i, c).wait_recv()
                    y_start(i, z_plan(i)[2], c)

                when(z_plan(i)[4], arrived)
        for i in range(noff):
            when(z_plan(i)[4], lambda i=i: z_copy(i, 2).wait_recv())

        def y_wait(i, slot, up):
            pl.when(has_high if up else has_low)(lambda: y_copy(i, slot, up).wait_send())
            pl.when(has_low if up else has_high)(lambda: y_copy(i, slot, up).wait_recv())

        for up in (0, 1):
            y_wait(noff, own, up)
            for i in range(noff):
                when(z_plan(i)[4], lambda i=i, up=up: y_wait(i, z_plan(i)[2], up))
        for c in range(3):
            for i in range(noff):
                when(z_plan(i)[3], lambda i=i, c=c: z_copy(i, c).wait_send())

        def group(c):
            return pl.ds(pl.multiple_of(c * 8, 8), 8)

        lane = lax.broadcasted_iota(jnp.int32, (8, cols), 1)

        def pack(c, _):
            for s in range(layers):
                total = jnp.zeros((8, cols), jnp.float32)
                for r in range(ext):
                    moved = pltpu.roll(xe[s, r, group(c), 0:cols], 8 * r, axis=1) if r else xe[
                        s, r, group(c), 0:cols
                    ]
                    shifted = lane + DEPTH if r == 0 else lane - (8 * r - DEPTH)
                    keep = (shifted >= 0) & (shifted < 2 * DEPTH)
                    if r == 0:
                        keep = (lane < DEPTH) | (lane >= cols - DEPTH)
                    total = jnp.where(keep, moved, total)
                xs[s, group(c), :] = total
            return 0

        lax.fori_loop(0, lead8 // 8, pack, 0)

        def x_copy(side):
            return pltpu.make_async_remote_copy(
                src_ref=xs,
                dst_ref=xr.at[side],
                send_sem=xsend.at[side],
                recv_sem=xrecv.at[side],
                device_id={"gx": x + 1 if side else x - 1},
                device_id_type=MESH,
            )

        sends = (x > 0, x < nx - 1)
        for side in (0, 1):
            pl.when(sends[side])(lambda side=side: x_copy(side).start())
        for side in (0, 1):
            pl.when(sends[side])(lambda side=side: x_copy(side).wait_send())
            pl.when(sends[1 - side])(lambda side=side: x_copy(side).wait_recv())

        near = (lane & 7) < 4
        rim = (lane < DEPTH) | (lane >= cols - DEPTH)

        def unpack(c, _):
            outside = jnp.where(c == leads // 8, -1.0, 0.0)
            for s in range(layers):
                both = jnp.where(near, xr[0, s, group(c), :], xr[1, s, group(c), :])
                for r in range(ext):
                    moved = pltpu.roll(both, cols - 8 * r, axis=1) if r else both
                    xe[s, r, group(c), cols : 2 * cols] = jnp.where(rim, moved, outside)
            return 0

        lax.fori_loop(0, lead8 // 8, unpack, 0)

        values = [[table[i, t] for t in range(table.shape[1])] for i in range(6)]

        def lookup(r, _):
            for s in range(layers):
                label = xe[s, r, leads:lead8, :]
                parts = [jnp.zeros(label.shape, jnp.float32)] * 6
                for t in range(table.shape[1]):
                    match = label == float(t)
                    parts = [jnp.where(match, values[i][t], parts[i]) for i in range(6)]
                for i in range(6):
                    coef[i, s, r] = parts[i]
                inside[s, r] = jnp.where(label >= 0.0, 1.0, 0.0)
            return 0

        lax.fori_loop(0, ext, lookup, 0)

        wide = 2 * cols
        lanes = lax.broadcasted_iota(jnp.int32, (8, wide), 1)
        column_id = x * cols + jnp.where(lanes >= cols + cols // 2, lanes - wide, lanes)

        def operate(source, emit, lo, hi, c):
            below_y = [None] * layers
            for r in range(lo - 1, hi):
                here = [source[s, r, group(c), :] for s in range(layers)]
                below_z = None
                for s in range(layers):
                    t = [coef[i, s, r] for i in range(6)]
                    v = here[s]
                    grad_x = pltpu.roll(v, wide - 1, axis=1) - v
                    grad_y = source[s, r + 1, group(c), :] - v
                    grad_z = here[s + 1] - v if s + 1 < layers else -v
                    flux_y = t[3] * grad_x + t[1] * grad_y + t[5] * grad_z
                    if r >= lo:
                        flux_x = t[0] * grad_x + t[3] * grad_y + t[4] * grad_z
                        flux_z = t[4] * grad_x + t[5] * grad_y + t[2] * grad_z
                        total = (below_y[s] - flux_y) + (pltpu.roll(flux_x, 1, axis=1) - flux_x)
                        total = total - flux_z if below_z is None else total + (below_z - flux_z)
                        emit(s, r, c, total * inside[s, r])
                        below_z = flux_z
                    below_y[s] = flux_y

        def emit_r(s, r, c, value):
            row_id = (first + s) * (ny * rows) + y * rows + (r - DEPTH)
            voxel = (row_id * (nx * cols) + column_id).astype(jnp.float32)
            source = jnp.where(elec[0, group(c), :] == voxel, 1.0, 0.0) - jnp.where(
                elec[1, group(c), :] == voxel, 1.0, 0.0
            )
            re[s, r, group(c), :] = source * inside[s, r] - value

        def emit_q(s, r, c, value):
            qe[s, r, group(c), :] = value

        def emit_p(s, r, c, value):
            xe[s, r, group(c), 0:cols] = value[:, 0:cols]

        def loop(source, emit, lo, hi):
            def step(c, _):
                operate(source, emit, lo, hi, c)
                return 0

            lax.fori_loop(0, leads // 8, step, 0)

        loop(xe, emit_r, 1, ext - 1)
        loop(re, emit_q, 2, ext - 2)
        loop(qe, emit_p, 3, ext - 3)
        for r in range(rows):
            at = slice(r * cols, (r + 1) * cols)
            base_out[0:leads, at] = re[own, DEPTH + r, :, 0:cols]
            base_out[leads : 2 * leads, at] = qe[own, DEPTH + r, :, 0:cols]
            base_out[2 * leads : 3 * leads, at] = xe[own, DEPTH + r, 0:leads, 0:cols]
        upper = nt_dot(base_out[0:leads, :], base_out[0 : 2 * leads, :])
        lower = nt_dot(base_out[leads : 2 * leads, :], base_out[leads : 3 * leads, :])
        grams = jnp.concatenate([upper, lower], axis=0)
        for i in range(plane):
            gs[i] = grams[i * share : (i + 1) * share, :]

        def a_copy(phase, k, src, dst, device):
            return pltpu.make_async_remote_copy(
                src_ref=src, dst_ref=dst,
                send_sem=asend.at[phase, k], recv_sem=arecv.at[phase, k],
                device_id=device, device_id_type=MESH,
            )

        def scatter(k):
            peer, device = plane_peer(k)
            return a_copy(0, k, gs.at[peer], rs.at[me], device)

        def along(k):
            return a_copy(1, k, zs.at[x], zs.at[x], {"gx": lax.rem(x + k, nx)})

        def gather(k):
            return a_copy(2, k, gram_out.at[me], gram_out.at[me], plane_peer(k)[1])

        def exchange(copy, count):
            for k in range(1, count):
                copy(k).start()
            for k in range(1, count):
                copy(k).wait()

        rs[me] = gs[me]
        exchange(scatter, plane)
        zs[x] = jnp.sum(rs[...], axis=0)
        exchange(along, nx)
        gram_out[me] = jnp.sum(zs[...], axis=0)
        exchange(gather, plane)

    vmem = pl.BlockSpec(memory_space=pltpu.VMEM)
    f32 = jnp.float32
    group_sems = pltpu.SemaphoreType.DMA((3, max(plane, nx)))
    call = pl.pallas_call(
        kernel,
        out_shape=(
            jax.ShapeDtypeStruct((3 * leads, rows * cols), f32),
            jax.ShapeDtypeStruct((plane, share, size), f32),
        ),
        in_specs=[pl.BlockSpec(memory_space=pltpu.SMEM), vmem, vmem, vmem],
        out_specs=(vmem, vmem),
        scratch_shapes=[
            pltpu.VMEM((layers, ext, lead8, 2 * cols), f32),
            pltpu.VMEM((layers, ext, leads, 2 * cols), f32),
            pltpu.VMEM((layers, ext, leads, 2 * cols), f32),
            pltpu.VMEM((6, layers, ext, 8, 2 * cols), f32),
            pltpu.VMEM((layers, ext, 8, 2 * cols), f32),
            pltpu.VMEM((2, leads, 2 * cols), f32),
            pltpu.VMEM((layers, lead8, cols), f32),
            pltpu.VMEM((2, layers, lead8, cols), f32),
            pltpu.VMEM((plane, share, size), f32),
            pltpu.VMEM((plane, share, size), f32),
            pltpu.VMEM((nx, share, size), f32),
            pltpu.SemaphoreType.DMA((noff, 3)),
            pltpu.SemaphoreType.DMA((noff, 3)),
            pltpu.SemaphoreType.DMA((noff + 1, 2)),
            pltpu.SemaphoreType.DMA((noff + 1, 2)),
            pltpu.SemaphoreType.DMA((2,)),
            pltpu.SemaphoreType.DMA((2,)),
            group_sems,
            group_sems,
        ],
        compiler_params=pltpu.CompilerParams(
            collective_id=0, has_side_effects=True,
            vmem_limit_bytes=(8 + 7 * layers) * 1024 * 1024,
        ),
        name="krylov",
    )
    return call, size


def eliminate(matrix, count):
    row_id = lax.broadcasted_iota(jnp.int32, (8, 1), 0)
    tiles = [matrix[i : i + 8, :] for i in range(0, count, 8)]
    for k in range(count):
        home, row = divmod(k, 8)
        source = tiles[home][row : row + 1, :]
        pivot = source * (1.0 / source[:, k : k + 1])
        tiles = [tile - tile[:, k : k + 1] * pivot if i != home else jnp.where(
            row_id == row, pivot, tile - tile[:, k : k + 1] * pivot
        ) for i, tile in enumerate(tiles)]
    return jnp.concatenate(tiles, axis=0)


def make_combine(leads, rows, cols):
    def kernel(gram, base, field, out, res):
        rr, rq = gram[0:leads, 0:leads], gram[0:leads, leads : 2 * leads]
        qq, qp = gram[leads : 2 * leads, 0:leads], gram[leads : 2 * leads, leads : 2 * leads]
        first = eliminate(jnp.concatenate([rq, rr, qq], axis=1), leads)
        z2, z1 = first[:, leads : 2 * leads], first[:, 2 * leads : 3 * leads]
        schur = jnp.concatenate([qp, rq], axis=1) - nn_dot(qq, jnp.concatenate([z1, z2], axis=1))
        e = eliminate(schur, leads)[:, leads : 2 * leads]
        c = z2 - nn_dot(z1, e)
        mix = jnp.transpose(jnp.concatenate([c, e], axis=0))
        gain = nn_dot(mix, base[0 : 2 * leads, :])
        loss = nn_dot(mix, base[leads : 3 * leads, :])
        for r in range(rows):
            at = slice(r * cols, (r + 1) * cols)
            spread = pl.ds(r, leads, stride=rows)
            out[spread, :] = field[spread, :] + gain[:, at]
            res[spread, :] = base[0:leads, at] - loss[:, at]

    vmem = pl.BlockSpec(memory_space=pltpu.VMEM)
    shape = jax.ShapeDtypeStruct((leads * rows, cols), jnp.float32)
    return pl.pallas_call(
        kernel,
        out_shape=(shape, shape),
        in_specs=[vmem] * 3,
        out_specs=(vmem, vmem),
        compiler_params=pltpu.CompilerParams(vmem_limit_bytes=24 * 1024 * 1024),
        name="combine",
    )


def solution(mesh):
    nz, ny, nx = (mesh.shape[name] for name in ("gz", "gy", "gx"))

    def body(labels, tissue_tensors, electrodes, initial):
        leads, _, rows, cols = initial.shape
        field = initial.reshape(leads * rows, cols)
        krylov, size = make_krylov(nz, ny, nx, leads, rows, cols)
        base, gram = krylov(tissue_tensors, labels.reshape(rows, cols), electrodes, field)
        out, res = make_combine(leads, rows, cols)(gram.reshape(size, size), base, field)
        return out.reshape(initial.shape), res.reshape(initial.shape)

    placed = (P("gz", "gy", "gx"), P(), P(), P(None, "gz", "gy", "gx"))
    return jax.shard_map(
        body,
        mesh=mesh,
        in_specs=placed,
        out_specs=(P(None, "gz", "gy", "gx"), P(None, "gz", "gy", "gx")),
        check_vma=False,
    )
```

time: 281 us -> 54.5 us (0.19)
  blocking collectives: 122 us -> 0 us
  starting transfers between devices: 52.4 us -> 0 us
  other arithmetic: 50.7 us -> 0 us
  Pallas kernels: 0 us -> 50.6 us
  waiting for transfers between devices: 25.3 us -> 0 us
  local copies, waits for them, and re-layouts: 22.4 us -> 3 us
  matrix products: 5.49 us -> 0 us
    psum x3 -> x0, blocking collectives: 122 us -> none  [the longest x1 42.6 us: body(): rr_now = lax.psum(gram_of(residual, residual), ('gz', 'gy', 'gx'))]
    ppermute x21 -> x0, starting transfers between devices: 52.4 us -> none  [the longest x9 31.5 us: padded_2(): lax.ppermute(lax.slice_in_dim(block, block.shape[dim] - width, None, axis...]
    pallas_call x0 -> x2, Pallas kernels: none -> 50.6 us  [the longest x1 37.7 us: body(): krylov(tissue_tensors, labels.reshape(rows, cols), electrodes, field)]
    another operation x15 -> x0, other arithmetic: 36.2 us -> none  [the longest x9 19.6 us: factor_solve(): factor = jnp.linalg.cholesky(matrix)]
    ppermute x21 -> x0, waiting for transfers between devices: 25.3 us -> none  [the longest x9 19.7 us: padded_2(): lax.ppermute(lax.slice_in_dim(block, 0, width, axis=dim), axis, backward)]
    ppermute x6 -> x0, local copies, waits for them, and re-layouts: 9.43 us -> none  [the longest x3 5.42 us: padded_2(): lax.ppermute(lax.slice_in_dim(block, 0, width, axis=dim), axis, backward)]
    add x11 -> x0, other arithmetic: 7.49 us -> none  [the longest x3 4.52 us: flux_terms(): flux_z = tensor[4] * grad_x + tensor[5] * grad_y + tensor[2] * grad_z]
    slice x13 -> x0, local copies, waits for them, and re-layouts: 6.31 us -> none  [the longest x6 3.28 us: padded_2(): lax.slice_in_dim(block, 0, width, axis=dim)]
  transfers between devices with their start and end apart: 21 -> 0, of which waited for: 10 -> 0; matrix products, arithmetic and copies ran while one was open for 6% -> 0% of each run, Pallas kernels for 0% -> 0%
where the time goes in v1:
time: 54.5 us; the launch traced here: 54.3 us
  Pallas kernels  50.6 us (93%)
  local copies, waits for them, and re-layouts  3 us (6%)
  between operations  0.66 us (1%)
    pallas_call x1, Pallas kernels, body(): krylov(tissue_tensors, labels.reshape(rows, cols), electrodes, field)  37.7 us
    pallas_call x1, Pallas kernels, body(): make_combine(leads, rows, cols)(gram.reshape(size, size), base, field)  12.9 us
    unnamed x10, local copies, waits for them, and re-layouts  3 us

profile of v1, /device:TPU:0, one launch (start us, length us, event | category | flops | bytes accessed | tf_op | source)
XLA Modules:
  0.0 54.3 jit_solution(9540649474846200491)
XLA Ops:
  0.6 0.0 copy-start.4
  0.6 0.7 %copy-done.4 = s32[2,64]{1,0:T(2,128)S(1)} copy-done((s32[2,64]{1,0:T(2,128)S(1)}, s32[2,64]{1,0:T(2,128)}, u32[]{:S(2)}) %copy-start.4) | copy-done | bytes 536
  1.3 0.0 copy-start
  1.3 0.9 %copy-done = f32[64,1,8,128]{3,2,1,0:T(8,128)S(1)} copy-done((f32[64,1,8,128]{3,2,1,0:T(8,128)S(1)}, f32[64,1,8,128]{3,2,1,0:T(8,128)}, u32[]{:S(2)}) %copy-start) | copy-done | bytes 262168
  2.3 0.0 copy-start.2
  2.3 0.7 %copy-done.2 = f32[6,8]{1,0:T(8,128)S(1)} copy-done((f32[6,8]{1,0:T(8,128)S(1)}, f32[6,8]{1,0:T(8,128)}, u32[]{:S(2)}) %copy-start.2) | copy-done | bytes 216
  2.9 0.0 copy-start.3
  3.0 0.7 %copy-done.3 = s32[1,8,128]{2,1,0:T(8,128)S(1)} copy-done((s32[1,8,128]{2,1,0:T(8,128)S(1)}, s32[1,8,128]{2,1,0:T(8,128)}, u32[]{:S(2)}) %copy-start.3) | copy-done | bytes 4120
  3.6 0.0 copy-start.1
  3.6 37.7 %krylov.1 = (f32[192,1024]{1,0:T(8,128)S(1)}, f32[8,16,128]{2,1,0:T(8,128)S(1)}) custom-call(f32[6,8]{1,0:T(8,128)S(1)} %copy-done.2, s32[8,128]{1,0:T(8,128)S(1)} %bitcast.12, s32[2,64]{1,0:T(2,128)S(1)} %copy-done.4, f32[512,128]{1,0:T(8,128)S(1)} %bitcast.9), custom_call_target="tpu_custom_call" | custom-call | tf_op jit(solution)/shard_map/krylov/pallas_call | solution.py:436
  41.4 0.0 copy-done.1
  41.4 12.9 %combine.1 = (f32[512,128]{1,0:T(8,128)}, f32[512,128]{1,0:T(8,128)}) custom-call(f32[128,128]{1,0:T(8,128)S(1)} %bitcast.11, f32[192,1024]{1,0:T(8,128)S(1)} %get-tuple-element.7.base, f32[512,128]{1,0:T(8,128)S(1)} %bitcast.10), custom_call_target="tpu_custom_call" | custom-call | tf_op jit(solution)/shard_map/combine/pallas_call | solution.py:437
Async XLA Ops:
  0.6 0.7 %copy-start.4 = (s32[2,64]{1,0:T(2,128)S(1)}, s32[2,64]{1,0:T(2,128)}, u32[]{:S(2)}) copy-start(s32[2,64]{1,0:T(2,128)} %electrodes.1) | copy-start | bytes 1540
  1.3 0.9 %copy-start = (f32[64,1,8,128]{3,2,1,0:T(8,128)S(1)}, f32[64,1,8,128]{3,2,1,0:T(8,128)}, u32[]{:S(2)}) copy-start(f32[64,1,8,128]{3,2,1,0:T(8,128)} %param.7) | copy-start | bytes 786436
  2.3 0.7 %copy-start.2 = (f32[6,8]{1,0:T(8,128)S(1)}, f32[6,8]{1,0:T(8,128)}, u32[]{:S(2)}) copy-start(f32[6,8]{1,0:T(8,128)} %table.1) | copy-start | bytes 580
  2.9 0.7 %copy-start.3 = (s32[1,8,128]{2,1,0:T(8,128)S(1)}, s32[1,8,128]{2,1,0:T(8,128)}, u32[]{:S(2)}) copy-start(s32[1,8,128]{2,1,0:T(8,128)} %param.4) | copy-start | bytes 12292
  3.6 37.8 %copy-start.1 = (f32[64,1,8,128]{3,2,1,0:T(8,128)S(1)}, f32[64,1,8,128]{3,2,1,0:T(8,128)}, u32[]{:S(2)}) copy-start(f32[64,1,8,128]{3,2,1,0:T(8,128)} %param.7) | copy-start | bytes 786436

commit v2 on v1

--- a/solution.py
+++ b/solution.py
@@ -22,7 +22,7 @@
     )
 
 
-def make_krylov(nz, ny, nx, leads, rows, cols):
+def make_krylov(nz, ny, nx, leads, rows, cols, classes):
     windowed = nz > DEPTH + 1
     layers = 2 * DEPTH + 1 if windowed else nz
     lead8 = leads + 8
@@ -38,7 +38,8 @@
     share = size // plane
 
     def kernel(
-        table, labels, electrodes, field, base_out, gram_out,
+        table_hbm, labels_hbm, electrodes_hbm, field_hbm, base_out, gram_out,
+        table, labels, electrodes, field, lsem,
         xe, re, qe, coef, inside, elec, xs, xr, gs, rs, zs,
         zsend, zrecv, ysend, yrecv, xsend, xrecv, asend, arecv,
     ):
@@ -51,6 +52,17 @@
             peer = lax.rem(me + k, plane)
             return peer, {"gz": peer // ny, "gy": lax.rem(peer, ny)}
 
+        loads = [
+            pltpu.make_async_copy(source, target, lsem.at[i])
+            for i, (source, target) in enumerate(
+                (
+                    (field_hbm, field), (labels_hbm, labels),
+                    (electrodes_hbm, electrodes), (table_hbm, table),
+                )
+            )
+        ]
+        for load in loads:
+            load.start()
         barrier = pltpu.get_barrier_semaphore()
         for k in range(1, plane):
             pl.semaphore_signal(
@@ -91,6 +103,8 @@
                     xr[side, s, 0:leads] = jnp.zeros((leads, cols), jnp.float32)
                     xr[side, s, leads:lead8] = jnp.full((8, cols), -1.0, jnp.float32)
 
+        for load in loads:
+            load.wait()
         for r in range(rows):
             xe[own, DEPTH + r, 0:leads, 0:cols] = field[pl.ds(r, leads, stride=rows), :]
             xe[own, DEPTH + r, leads:lead8, 0:cols] = jnp.broadcast_to(
@@ -144,9 +158,12 @@
         def y_start(i, slot, up):
             pl.when(has_high if up else has_low)(lambda: y_copy(i, slot, up).start())
 
-        for c in range(3):
+        def z_start(c):
             for i in range(noff):
-                when(z_plan(i)[3], lambda i=i, c=c: z_copy(i, c).start())
+                when(z_plan(i)[3], lambda i=i: z_copy(i, c).start())
+
+        z_start(0)
+        z_start(1)
         for up in (0, 1):
             y_start(noff, own, up)
 
@@ -168,6 +185,8 @@
                     y_start(i, z_plan(i)[2], c)
 
                 when(z_plan(i)[4], arrived)
+            if c == 0:
+                z_start(2)
         for i in range(noff):
             when(z_plan(i)[4], lambda i=i: z_copy(i, 2).wait_recv())
 
@@ -351,9 +370,14 @@
             jax.ShapeDtypeStruct((3 * leads, rows * cols), f32),
             jax.ShapeDtypeStruct((plane, share, size), f32),
         ),
-        in_specs=[pl.BlockSpec(memory_space=pltpu.SMEM), vmem, vmem, vmem],
+        in_specs=[pl.BlockSpec(memory_space=pltpu.HBM)] * 4,
         out_specs=(vmem, vmem),
         scratch_shapes=[
+            pltpu.SMEM((6, classes), f32),
+            pltpu.VMEM((rows, cols), jnp.int32),
+            pltpu.VMEM((2, leads), jnp.int32),
+            pltpu.VMEM((leads * rows, cols), f32),
+            pltpu.SemaphoreType.DMA((4,)),
             pltpu.VMEM((layers, ext, lead8, 2 * cols), f32),
             pltpu.VMEM((layers, ext, leads, 2 * cols), f32),
             pltpu.VMEM((layers, ext, leads, 2 * cols), f32),
@@ -385,14 +409,24 @@
 
 def eliminate(matrix, count):
     row_id = lax.broadcasted_iota(jnp.int32, (8, 1), 0)
+    matrix = matrix * (1.0 / matrix[0:1, 0:1])
     tiles = [matrix[i : i + 8, :] for i in range(0, count, 8)]
-    for k in range(count):
+    for k in range(0, count, 2):
         home, row = divmod(k, 8)
-        source = tiles[home][row : row + 1, :]
-        pivot = source * (1.0 / source[:, k : k + 1])
-        tiles = [tile - tile[:, k : k + 1] * pivot if i != home else jnp.where(
-            row_id == row, pivot, tile - tile[:, k : k + 1] * pivot
-        ) for i, tile in enumerate(tiles)]
+        one, two = tiles[home][row : row + 1, :], tiles[home][row + 1 : row + 2, :]
+        left = [jnp.broadcast_to(tile[:, k : k + 1], tile.shape) for tile in tiles]
+        right = [jnp.broadcast_to(tile[:, k + 1 : k + 2], tile.shape) for tile in tiles]
+        p11, p21 = left[home][row : row + 1, :], left[home][row + 1 : row + 2, :]
+        p12, p22 = right[home][row : row + 1, :], right[home][row + 1 : row + 2, :]
+        inverse = 1.0 / (p11 * p22 - p12 * p21)
+        first = (p22 * inverse) * one - (p12 * inverse) * two
+        second = (p11 * inverse) * two - (p21 * inverse) * one
+        tiles = [
+            tile - left[i] * first - right[i] * second for i, tile in enumerate(tiles)
+        ]
+        tiles[home] = jnp.where(
+            row_id == row, first, jnp.where(row_id == row + 1, second, tiles[home])
+        )
     return jnp.concatenate(tiles, axis=0)
 
 
@@ -432,7 +466,9 @@
     def body(labels, tissue_tensors, electrodes, initial):
         leads, _, rows, cols = initial.shape
         field = initial.reshape(leads * rows, cols)
-        krylov, size = make_krylov(nz, ny, nx, leads, rows, cols)
+        krylov, size = make_krylov(
+            nz, ny, nx, leads, rows, cols, tissue_tensors.shape[1]
+        )
         base, gram = krylov(tissue_tensors, labels.reshape(rows, cols), electrodes, field)
         out, res = make_combine(leads, rows, cols)(gram.reshape(size, size), base, field)
         return out.reshape(initial.shape), res.reshape(initial.shape)

time: 54.5 us -> 49.8 us (0.914)
  Pallas kernels: 50.6 us -> 45.9 us
    pallas_call x1, Pallas kernels: 12.9 us -> 8.61 us  [body(): make_combine(leads, rows, cols)(gram.reshape(size, size), base, field)]
where the time goes in v2:
time: 49.8 us; the launch traced here: 49.6 us
  Pallas kernels  45.9 us (92%)
  local copies, waits for them, and re-layouts  3 us (6%)
  between operations  0.66 us (1%)
    pallas_call x1, Pallas kernels, body(): krylov(tissue_tensors, labels.reshape(rows, cols), electrodes, field)  37.3 us
    pallas_call x1, Pallas kernels, body(): make_combine(leads, rows, cols)(gram.reshape(size, size), base, field)  8.61 us
    unnamed x10, local copies, waits for them, and re-layouts  3 us

profile of v2, /device:TPU:0, one launch (start us, length us, event | category | flops | bytes accessed | tf_op | source)
XLA Modules:
  0.0 49.6 jit_solution(11061097149023874177)
XLA Ops:
  0.6 0.0 copy-start.4
  0.6 0.7 %copy-done.4 = s32[2,64]{1,0:T(2,128)S(1)} copy-done((s32[2,64]{1,0:T(2,128)S(1)}, s32[2,64]{1,0:T(2,128)}, u32[]{:S(2)}) %copy-start.4) | copy-done | bytes 536
  1.3 0.0 copy-start
  1.3 0.9 %copy-done = f32[64,1,8,128]{3,2,1,0:T(8,128)S(1)} copy-done((f32[64,1,8,128]{3,2,1,0:T(8,128)S(1)}, f32[64,1,8,128]{3,2,1,0:T(8,128)}, u32[]{:S(2)}) %copy-start) | copy-done | bytes 262168
  2.3 0.0 copy-start.2
  2.3 0.7 %copy-done.2 = f32[6,8]{1,0:T(8,128)S(1)} copy-done((f32[6,8]{1,0:T(8,128)S(1)}, f32[6,8]{1,0:T(8,128)}, u32[]{:S(2)}) %copy-start.2) | copy-done | bytes 216
  2.9 0.0 copy-start.3
  3.0 0.7 %copy-done.3 = s32[1,8,128]{2,1,0:T(8,128)S(1)} copy-done((s32[1,8,128]{2,1,0:T(8,128)S(1)}, s32[1,8,128]{2,1,0:T(8,128)}, u32[]{:S(2)}) %copy-start.3) | copy-done | bytes 4120
  3.6 0.0 copy-start.1
  3.6 37.3 %krylov.1 = (f32[192,1024]{1,0:T(8,128)S(1)}, f32[8,16,128]{2,1,0:T(8,128)S(1)}) custom-call(f32[6,8]{1,0:T(8,128)S(1)} %copy-done.2, s32[8,128]{1,0:T(8,128)S(1)} %bitcast.12, s32[2,64]{1,0:T(2,128)S(1)} %copy-done.4, f32[512,128]{1,0:T(8,128)S(1)} %bitcast.9), custom_call_target="tpu_custom_call" | custom-call | tf_op jit(solution)/shard_map/krylov/pallas_call | solution.py:472
  41.0 0.0 copy-done.1
  41.0 8.6 %combine.1 = (f32[512,128]{1,0:T(8,128)}, f32[512,128]{1,0:T(8,128)}) custom-call(f32[128,128]{1,0:T(8,128)S(1)} %bitcast.11, f32[192,1024]{1,0:T(8,128)S(1)} %get-tuple-element.7.base, f32[512,128]{1,0:T(8,128)S(1)} %bitcast.10), custom_call_target="tpu_custom_call" | custom-call | tf_op jit(solution)/shard_map/combine/pallas_call | solution.py:473
Async XLA Ops:
  0.6 0.7 %copy-start.4 = (s32[2,64]{1,0:T(2,128)S(1)}, s32[2,64]{1,0:T(2,128)}, u32[]{:S(2)}) copy-start(s32[2,64]{1,0:T(2,128)} %electrodes_hbm.1) | copy-start | bytes 1540
  1.3 0.9 %copy-start = (f32[64,1,8,128]{3,2,1,0:T(8,128)S(1)}, f32[64,1,8,128]{3,2,1,0:T(8,128)}, u32[]{:S(2)}) copy-start(f32[64,1,8,128]{3,2,1,0:T(8,128)} %param.7) | copy-start | bytes 786436
  2.3 0.7 %copy-start.2 = (f32[6,8]{1,0:T(8,128)S(1)}, f32[6,8]{1,0:T(8,128)}, u32[]{:S(2)}) copy-start(f32[6,8]{1,0:T(8,128)} %table_hbm.1) | copy-start | bytes 580
  2.9 0.7 %copy-start.3 = (s32[1,8,128]{2,1,0:T(8,128)S(1)}, s32[1,8,128]{2,1,0:T(8,128)}, u32[]{:S(2)}) copy-start(s32[1,8,128]{2,1,0:T(8,128)} %param.4) | copy-start | bytes 12292
  3.6 37.3 %copy-start.1 = (f32[64,1,8,128]{3,2,1,0:T(8,128)S(1)}, f32[64,1,8,128]{3,2,1,0:T(8,128)}, u32[]{:S(2)}) copy-start(f32[64,1,8,128]{3,2,1,0:T(8,128)} %param.7) | copy-start | bytes 786436

commit v3 on v2

--- a/solution.py
+++ b/solution.py
@@ -177,6 +177,55 @@
             )
             elec[e] = jnp.broadcast_to(column, (leads, 2 * cols))
 
+        def y_wait(i, slot, up):
+            pl.when(has_high if up else has_low)(lambda: y_copy(i, slot, up).wait_send())
+            pl.when(has_low if up else has_high)(lambda: y_copy(i, slot, up).wait_recv())
+
+        def group(c):
+            return pl.ds(pl.multiple_of(c * 8, 8), 8)
+
+        lane = lax.broadcasted_iota(jnp.int32, (8, cols), 1)
+
+        def pack(c, s):
+            total = jnp.zeros((8, cols), jnp.float32)
+            for r in range(ext):
+                moved = pltpu.roll(xe[s, r, group(c), 0:cols], 8 * r, axis=1) if r else xe[
+                    s, r, group(c), 0:cols
+                ]
+                shifted = lane + DEPTH if r == 0 else lane - (8 * r - DEPTH)
+                keep = (shifted >= 0) & (shifted < 2 * DEPTH)
+                if r == 0:
+                    keep = (lane < DEPTH) | (lane >= cols - DEPTH)
+                total = jnp.where(keep, moved, total)
+            xs[s, group(c), :] = total
+            return s
+
+        def x_copy(side, i, slot):
+            return pltpu.make_async_remote_copy(
+                src_ref=xs.at[slot],
+                dst_ref=xr.at[side, slot],
+                send_sem=xsend.at[side, i],
+                recv_sem=xrecv.at[side, i],
+                device_id={"gx": x + 1 if side else x - 1},
+                device_id_type=MESH,
+            )
+
+        sends = (x > 0, x < nx - 1)
+
+        def x_start(i, slot):
+            lax.fori_loop(0, lead8 // 8, pack, slot)
+            for side in (0, 1):
+                pl.when(sends[side])(lambda side=side: x_copy(side, i, slot).start())
+
+        def x_wait(i, slot):
+            for side in (0, 1):
+                pl.when(sends[side])(lambda side=side: x_copy(side, i, slot).wait_send())
+                pl.when(sends[1 - side])(lambda side=side: x_copy(side, i, slot).wait_recv())
+
+        for up in (0, 1):
+            y_wait(noff, own, up)
+        x_start(noff, own)
+
         for c in range(2):
             for i in range(noff):
 
@@ -190,56 +239,17 @@
         for i in range(noff):
             when(z_plan(i)[4], lambda i=i: z_copy(i, 2).wait_recv())
 
-        def y_wait(i, slot, up):
-            pl.when(has_high if up else has_low)(lambda: y_copy(i, slot, up).wait_send())
-            pl.when(has_low if up else has_high)(lambda: y_copy(i, slot, up).wait_recv())
-
         for up in (0, 1):
-            y_wait(noff, own, up)
             for i in range(noff):
                 when(z_plan(i)[4], lambda i=i, up=up: y_wait(i, z_plan(i)[2], up))
+        for i in range(noff):
+            x_start(i, z_plan(i)[2])
         for c in range(3):
             for i in range(noff):
                 when(z_plan(i)[3], lambda i=i, c=c: z_copy(i, c).wait_send())
-
-        def group(c):
-            return pl.ds(pl.multiple_of(c * 8, 8), 8)
-
-        lane = lax.broadcasted_iota(jnp.int32, (8, cols), 1)
-
-        def pack(c, _):
-            for s in range(layers):
-                total = jnp.zeros((8, cols), jnp.float32)
-                for r in range(ext):
-                    moved = pltpu.roll(xe[s, r, group(c), 0:cols], 8 * r, axis=1) if r else xe[
-                        s, r, group(c), 0:cols
-                    ]
-                    shifted = lane + DEPTH if r == 0 else lane - (8 * r - DEPTH)
-                    keep = (shifted >= 0) & (shifted < 2 * DEPTH)
-                    if r == 0:
-                        keep = (lane < DEPTH) | (lane >= cols - DEPTH)
-                    total = jnp.where(keep, moved, total)
-                xs[s, group(c), :] = total
-            return 0
-
-        lax.fori_loop(0, lead8 // 8, pack, 0)
-
-        def x_copy(side):
-            return pltpu.make_async_remote_copy(
-                src_ref=xs,
-                dst_ref=xr.at[side],
-                send_sem=xsend.at[side],
-                recv_sem=xrecv.at[side],
-                device_id={"gx": x + 1 if side else x - 1},
-                device_id_type=MESH,
-            )
-
-        sends = (x > 0, x < nx - 1)
-        for side in (0, 1):
-            pl.when(sends[side])(lambda side=side: x_copy(side).start())
-        for side in (0, 1):
-            pl.when(sends[side])(lambda side=side: x_copy(side).wait_send())
-            pl.when(sends[1 - side])(lambda side=side: x_copy(side).wait_recv())
+        x_wait(noff, own)
+        for i in range(noff):
+            x_wait(i, z_plan(i)[2])
 
         near = (lane & 7) < 4
         rim = (lane < DEPTH) | (lane >= cols - DEPTH)
@@ -393,8 +403,8 @@
             pltpu.SemaphoreType.DMA((noff, 3)),
             pltpu.SemaphoreType.DMA((noff + 1, 2)),
             pltpu.SemaphoreType.DMA((noff + 1, 2)),
-            pltpu.SemaphoreType.DMA((2,)),
-            pltpu.SemaphoreType.DMA((2,)),
+            pltpu.SemaphoreType.DMA((2, noff + 1)),
+            pltpu.SemaphoreType.DMA((2, noff + 1)),
             group_sems,
             group_sems,
         ],

time: 49.8 us -> 49.3 us (0.990)
  Pallas kernels: 45.9 us -> 45.4 us
    pallas_call x1, Pallas kernels: 37.3 us -> 36.8 us  [body(): krylov(tissue_tensors, labels.reshape(rows, cols), electrodes, field)]
where the time goes in v3:
time: 49.3 us; the launch traced here: 49 us
  Pallas kernels  45.4 us (92%)
  local copies, waits for them, and re-layouts  3 us (6%)
  between operations  0.66 us (1%)
    pallas_call x1, Pallas kernels, body(): krylov(tissue_tensors, labels.reshape(rows, cols), electrodes, field)  36.8 us
    pallas_call x1, Pallas kernels, body(): make_combine(leads, rows, cols)(gram.reshape(size, size), base, field)  8.61 us
    unnamed x10, local copies, waits for them, and re-layouts  3 us

profile of v3, /device:TPU:0, one launch (start us, length us, event | category | flops | bytes accessed | tf_op | source)
XLA Modules:
  0.0 49.0 jit_solution(2669460004839048469)
XLA Ops:
  0.6 0.0 copy-start.4
  0.6 0.7 %copy-done.4 = s32[2,64]{1,0:T(2,128)S(1)} copy-done((s32[2,64]{1,0:T(2,128)S(1)}, s32[2,64]{1,0:T(2,128)}, u32[]{:S(2)}) %copy-start.4) | copy-done | bytes 536
  1.3 0.0 copy-start
  1.3 0.9 %copy-done = f32[64,1,8,128]{3,2,1,0:T(8,128)S(1)} copy-done((f32[64,1,8,128]{3,2,1,0:T(8,128)S(1)}, f32[64,1,8,128]{3,2,1,0:T(8,128)}, u32[]{:S(2)}) %copy-start) | copy-done | bytes 262168
  2.3 0.0 copy-start.2
  2.3 0.7 %copy-done.2 = f32[6,8]{1,0:T(8,128)S(1)} copy-done((f32[6,8]{1,0:T(8,128)S(1)}, f32[6,8]{1,0:T(8,128)}, u32[]{:S(2)}) %copy-start.2) | copy-done | bytes 216
  2.9 0.0 copy-start.3
  3.0 0.7 %copy-done.3 = s32[1,8,128]{2,1,0:T(8,128)S(1)} copy-done((s32[1,8,128]{2,1,0:T(8,128)S(1)}, s32[1,8,128]{2,1,0:T(8,128)}, u32[]{:S(2)}) %copy-start.3) | copy-done | bytes 4120
  3.6 0.0 copy-start.1
  3.6 36.8 %krylov.1 = (f32[192,1024]{1,0:T(8,128)S(1)}, f32[8,16,128]{2,1,0:T(8,128)S(1)}) custom-call(f32[6,8]{1,0:T(8,128)S(1)} %copy-done.2, s32[8,128]{1,0:T(8,128)S(1)} %bitcast.12, s32[2,64]{1,0:T(2,128)S(1)} %copy-done.4, f32[512,128]{1,0:T(8,128)S(1)} %bitcast.9), custom_call_target="tpu_custom_call" | custom-call | tf_op jit(solution)/shard_map/krylov/pallas_call | solution.py:482
  40.4 0.0 copy-done.1
  40.4 8.6 %combine.1 = (f32[512,128]{1,0:T(8,128)}, f32[512,128]{1,0:T(8,128)}) custom-call(f32[128,128]{1,0:T(8,128)S(1)} %bitcast.11, f32[192,1024]{1,0:T(8,128)S(1)} %get-tuple-element.7.base, f32[512,128]{1,0:T(8,128)S(1)} %bitcast.10), custom_call_target="tpu_custom_call" | custom-call | tf_op jit(solution)/shard_map/combine/pallas_call | solution.py:483
Async XLA Ops:
  0.6 0.7 %copy-start.4 = (s32[2,64]{1,0:T(2,128)S(1)}, s32[2,64]{1,0:T(2,128)}, u32[]{:S(2)}) copy-start(s32[2,64]{1,0:T(2,128)} %electrodes_hbm.1) | copy-start | bytes 1540
  1.3 0.9 %copy-start = (f32[64,1,8,128]{3,2,1,0:T(8,128)S(1)}, f32[64,1,8,128]{3,2,1,0:T(8,128)}, u32[]{:S(2)}) copy-start(f32[64,1,8,128]{3,2,1,0:T(8,128)} %param.7) | copy-start | bytes 786436
  2.3 0.7 %copy-start.2 = (f32[6,8]{1,0:T(8,128)S(1)}, f32[6,8]{1,0:T(8,128)}, u32[]{:S(2)}) copy-start(f32[6,8]{1,0:T(8,128)} %table_hbm.1) | copy-start | bytes 580
  2.9 0.7 %copy-start.3 = (s32[1,8,128]{2,1,0:T(8,128)S(1)}, s32[1,8,128]{2,1,0:T(8,128)}, u32[]{:S(2)}) copy-start(s32[1,8,128]{2,1,0:T(8,128)} %param.4) | copy-start | bytes 12292
  3.6 36.8 %copy-start.1 = (f32[64,1,8,128]{3,2,1,0:T(8,128)S(1)}, f32[64,1,8,128]{3,2,1,0:T(8,128)}, u32[]{:S(2)}) copy-start(f32[64,1,8,128]{3,2,1,0:T(8,128)} %param.7) | copy-start | bytes 786436
